TPU v7x, 32 devices: a whole 2x2x4 slice. The times are simulated.
32 devices in a mesh: stream: 2 (over y), seq: 8 (over z, core), tensor: 2 (over x).
Axes of the slice: x: 2, y: 2, z: 4, core: 2. Of those that a mesh axis runs over, the one named last changes fastest.
Arguments:
- hidden: bfloat16 [2, 1, 4096, 4096], P('stream', None, 'seq', 'tensor'), may hold values from -32 to 32
- norm_gain: float32 [4096], replicated, may hold values from 0.1 to 1.9
- query_weight: bfloat16 [4096, 4096], P('seq', 'tensor'), may hold values from -1 to 1
- key_weight: bfloat16 [4096, 1024], P('seq', 'tensor'), may hold values from -24 to 24
- value_projection_weight: bfloat16 [4096, 1024], P('seq', 'tensor'), may hold values from -0.09375 to 0.09375
- out_weight: bfloat16 [4096, 4096], P('tensor', 'seq'), may hold values from -0.125 to 0.125
Outputs:
- cross_out: bfloat16 [2, 1, 4096, 4096], P('stream', None, 'seq', 'tensor')
All inputs are finite; a program needn't handle non-finite values.
Results may differ from a plain program's by a relative error of at most 0.014.
The roundings to bfloat16 on the way count: a program that leaves them out, or rounds other values in their place, can miss the bound.
Values may be sent and summed in bfloat16 or wider, within the bound.
A program may use at most 256 MiB of HBM per device.

v0:
```python
import jax
import jax.numpy as jnp
from jax import lax
from jax.sharding import PartitionSpec as P

HEAD_DIM = 128


def swapped(block, axis, stride):
    count = lax.axis_size(axis)
    route = []
    for low in range(count):
        high = low | 1 << stride
        if high != low and high < count:
            route += [(low, high), (high, low)]
    return lax.ppermute(block, axis, route)


def online_update(running, query_heads, key_block, value_block, query_frame):
    maximum, totals, accumulated = running
    windows, key_count, key_width = key_block.shape
    heads_kv = query_heads.shape[1]
    head_size = query_heads.shape[3]
    key_heads = key_block.reshape(windows, key_count, heads_kv, head_size)
    value_heads = value_block.reshape(windows, key_count, heads_kv, head_size)
    scores = jnp.einsum(
        "bkrd,bnkd->bkrn", query_heads, key_heads, preferred_element_type=jnp.float32
    ) * head_size ** (-0.5)
    key_frame = jnp.arange(key_count, dtype=jnp.int32)
    allowed = key_frame[None, :] <= query_frame[:, None]
    scores = jnp.where(allowed, scores, -1e30)
    fresh = jnp.maximum(maximum, jnp.max(scores, axis=-1))
    expo = jnp.where(allowed, jnp.exp(scores - fresh[..., None]), 0.0)
    totals = jnp.sum(expo, axis=-1)
    product = jnp.einsum(
        "bkrn,bnkd->bkrd",
        expo.astype(jnp.bfloat16),
        value_heads,
        preferred_element_type=jnp.float32,
    )
    accumulated = product
    return (fresh, totals, accumulated)


def body(hidden, norm_gain, query_weight, key_weight, value_projection_weight, out_weight):
    windows = hidden.shape[1]
    frame_count = hidden.shape[2]
    gathered = lax.all_gather(hidden, "tensor", axis=3, tiled=True)
    model_width = gathered.shape[3]
    flat_rows = gathered.reshape(windows * frame_count, model_width).astype(jnp.float32)
    inverse_rms = lax.rsqrt(jnp.mean(flat_rows * flat_rows, axis=1, keepdims=True) + 1e-05)
    normed = (flat_rows * inverse_rms * norm_gain).astype(jnp.bfloat16)
    full_query, full_key, full_value, full_out = (
        lax.all_gather(query_weight, "seq", axis=0, tiled=True),
        lax.all_gather(key_weight, "seq", axis=0, tiled=True),
        lax.all_gather(value_projection_weight, "seq", axis=0, tiled=True),
        lax.all_gather(out_weight, "seq", axis=1, tiled=True),
    )
    query_sum = jnp.dot(normed, full_query, preferred_element_type=jnp.float32)
    key_sum = jnp.dot(normed, full_key, preferred_element_type=jnp.float32)
    value_sum = jnp.dot(normed, full_value, preferred_element_type=jnp.float32)
    query_rows = query_sum.astype(jnp.bfloat16)
    self_key_rows = key_sum.astype(jnp.bfloat16).reshape(windows, frame_count, key_weight.shape[1])
    self_value_rows = value_sum.astype(jnp.bfloat16).reshape(
        windows, frame_count, value_projection_weight.shape[1]
    )
    partner_keys, partner_values = swapped((self_key_rows, self_value_rows), "stream", 0)
    heads_kv = key_weight.shape[1] // HEAD_DIM
    group_repeat = query_weight.shape[1] // (heads_kv * HEAD_DIM)
    query_heads = (
        query_rows.reshape(windows, frame_count, heads_kv, group_repeat, HEAD_DIM)
        .transpose(0, 2, 3, 1, 4)
        .reshape(windows, heads_kv, group_repeat * frame_count, HEAD_DIM)
    )
    query_start = lax.axis_index("seq") * frame_count
    query_frame = query_start + jnp.tile(jnp.arange(frame_count, dtype=jnp.int32), group_repeat)
    initial = (
        jnp.full((windows, heads_kv, group_repeat * frame_count), -1e30, jnp.float32),
        jnp.zeros((windows, heads_kv, group_repeat * frame_count), jnp.float32),
        jnp.zeros((windows, heads_kv, group_repeat * frame_count, HEAD_DIM), jnp.float32),
    )
    query_end = query_start + frame_count
    pieces = (
        lax.all_gather(partner_keys, "seq", axis=1, tiled=True),
        lax.all_gather(partner_values, "seq", axis=1, tiled=True),
    )

    def taken(current):
        return online_update(current, query_heads, pieces[0], pieces[1], query_frame)

    def skipped(current):
        return current

    maximum, totals, accumulated = lax.cond(jnp.int32(0) < query_end, taken, skipped, initial)
    attended_output = (accumulated / totals[..., None]).astype(jnp.bfloat16)
    attended_output = (
        attended_output.reshape(windows, heads_kv, group_repeat, frame_count, HEAD_DIM)
        .transpose(0, 3, 1, 2, 4)
        .reshape(windows * frame_count, heads_kv * group_repeat * HEAD_DIM)
    )
    partial_out = jnp.dot(attended_output, full_out, preferred_element_type=jnp.float32)
    summed = lax.psum_scatter(
        partial_out.astype(jnp.bfloat16), "tensor", scatter_dimension=1, tiled=True
    ).astype(jnp.float32)
    return summed.astype(jnp.bfloat16).reshape(1, windows, frame_count, summed.shape[1])


def solution(mesh):
    in_specs = (
        P("stream", None, "seq", "tensor"),
        P(),
        P("seq", "tensor"),
        P("seq", "tensor"),
        P("seq", "tensor"),
        P("tensor", "seq"),
    )
    out_specs = P("stream", None, "seq", "tensor")
    return jax.shard_map(body, mesh=mesh, in_specs=in_specs, out_specs=out_specs, check_vma=False)
```

profile of v0, /device:TPU:0, one launch (start us, length us, event | category | flops | bytes accessed | tf_op | source)
XLA Modules:
  0.0 665.1 jit_solution(13722145855826253714)
XLA Ops:
  9.4 59.0 %all-gather.8.cloned.1.call-done = bf16[1,1,512,4096]{3,2,1,0:T(8,128)(2,1)} async-done(((bf16[1,1,512,2048]{3,2,1,0:T(8,128)(2,1)}), bf16[1,1,512,4096]{3,2,1,0:T(8,128)(2,1)}) %all-gather.8.cloned.1.call-update) | async-done | bytes 4194320 | tf_op jit(solution)/shard_map/all_gather | solution.py:48
  68.4 3.1 fusion.17
  71.5 45.7 %all-gather.12.cloned.1.call-done = bf16[4096,512]{1,0:T(8,128)(2,1)} async-done(((bf16[512,512]{1,0:T(8,128)(2,1)}), bf16[4096,512]{1,0:T(8,128)(2,1)}) %all-gather.12.cloned.1.call-update) | async-done | bytes 4194320 | tf_op jit(solution)/shard_map/all_gather | solution.py:55
  117.2 5.8 fusion.20
  124.6 12.6 %collective-permute-done = bf16[1,512,512]{2,1,0:T(8,128)(2,1)S(1)} collective-permute-done((bf16[1,512,512]{2,1,0:T(8,128)(2,1)S(1)}, bf16[1,512,512]{2,1,0:T(8,128)(2,1)S(1)}, u32[]{:S(2)}, u32[]{:S(2)}) %collective-permute-start) | collective-permute-done | bytes 524320 | tf_op jit(solution)/shard_map/ppermute | solution.py:16
  138.0 26.6 %all-gather.16.cloned.1.call-done = bf16[4096,512]{1,0:T(8,128)(2,1)} async-done(((bf16[512,512]{1,0:T(8,128)(2,1)}), bf16[4096,512]{1,0:T(8,128)(2,1)}) %all-gather.16.cloned.1.call-update) | async-done | bytes 4194320 | tf_op jit(solution)/shard_map/all_gather | solution.py:56
  164.7 5.8 fusion.21
  172.1 12.6 %collective-permute-done.1 = bf16[1,512,512]{2,1,0:T(8,128)(2,1)S(1)} collective-permute-done((bf16[1,512,512]{2,1,0:T(8,128)(2,1)S(1)}, bf16[1,512,512]{2,1,0:T(8,128)(2,1)S(1)}, u32[]{:S(2)}, u32[]{:S(2)}) %collective-permute-start.1) | collective-permute-done | bytes 524320 | tf_op jit(solution)/shard_map/ppermute | solution.py:16
  186.5 129.5 %all-gather.10.cloned.1.call-done = bf16[4096,2048]{1,0:T(8,128)(2,1)} async-done(((bf16[512,2048]{1,0:T(8,128)(2,1)}), bf16[4096,2048]{1,0:T(8,128)(2,1)}) %all-gather.10.cloned.1.call-update) | async-done | bytes 16777232 | tf_op jit(solution)/shard_map/all_gather | solution.py:54
  316.0 14.6 %convolution_convert_fusion.1 = bf16[512,2048]{1,0:T(8,128)(2,1)} fusion(bf16[4096,2048]{1,0:T(8,128)(2,1)} %all-gather.10.cloned.1.call-done, bf16[1,1,512,4096]{3,2,1,0:T(8,128)(2,1)} %all-gather.8.cloned.1.call-done, f32[4096]{0:T(1024)S(1)} %copy-done.3, f32[512]{0:T(512)S(1)} %add_rsqrt_fusion), kind=kOutput, calls=%fused_computation.24 | convolution fusion | flops 8599371776 | bytes 23087104 | tf_op jit(solution)/shard_map/dot_general | solution.py:59
  330.6 3.2 reshape.72
  335.7 27.1 %all-gather.14.cloned.1.call-done = bf16[1,4096,512]{2,1,0:T(8,128)(2,1)} async-done(((bf16[1,512,512]{2,1,0:T(8,128)(2,1)}), bf16[1,4096,512]{2,1,0:T(8,128)(2,1)}) %all-gather.14.cloned.1.call-update) | async-done | bytes 4194320 | tf_op jit(solution)/shard_map/all_gather | solution.py:84
  362.8 47.4 %all-gather.18.cloned.1.call-done = bf16[1,4096,512]{2,1,0:T(8,128)(2,1)} async-done(((bf16[1,512,512]{2,1,0:T(8,128)(2,1)}), bf16[1,4096,512]{2,1,0:T(8,128)(2,1)}) %all-gather.18.cloned.1.call-update) | async-done | bytes 4194320 | tf_op jit(solution)/shard_map/all_gather | solution.py:85
  410.2 174.7 %conditional.1 = (f32[1,4,2048]{2,1,0:T(4,128)}, f32[1,4,2048,128]{3,2,1,0:T(8,128)}) conditional(s32[]{:T(128)} %convert_element_type.33, () %tuple.13, (s32[]{:T(128)}, s32[4,512]{1,0:T(4,128)S(1)}, bf16[1,4,4,512,128]{4,3,2,1,0:T(8,128)(2,1)}, bf16[1,4096,512]{2,1,0:T(8,128)(2,1)}, bf16[1,4096,512]{2,1,0:T(8,128)(2,1)}) %tuple.34), branch_computations={%region_1.0_spmd, %region_2.5_spmd} | conditional | flops 17624459264 | bytes 476291136 | solution.py:94
  410.2 11.0 %iota_compare_fusion = pred[2048,4096]{1,0:T(8,128)(4,1)} fusion(s32[2048]{0:T(1024)S(1)} %bitcast.37), kind=kLoop, calls=%fused_computation.7 | loop fusion | flops 8388608 | bytes 8396800 | tf_op jit(solution)/shard_map/cond/branch_1_fun/le | solution.py:30
  421.2 7.1 %reshape.64 = bf16[4096,4,128]{2,1,0:T(4,128)(2,1)} reshape(bf16[1,4096,512]{2,1,0:T(8,128)(2,1)} %get-tuple-element.22) | data formatting | bytes 8388608 | tf_op jit(solution)/shard_map/reshape.1
  428.3 51.1 %fusion = (f32[4,2048]{1,0:T(4,128)S(1)}, f32[4,2048,4096]{2,1,0:T(8,128)}) fusion(pred[2048,4096]{1,0:T(8,128)(4,1)} %iota_compare_fusion, bf16[4,2048,128]{2,1,0:T(8,128)(2,1)S(1)} %bitcast.35, bf16[4096,4,128]{2,1,0:T(4,128)(2,1)} %reshape.64), kind=kOutput, calls=%fused_computation.2 | convolution fusion | flops 8690589696 | bytes 148930560 | tf_op jit(solution)/shard_map/cond/branch_1_fun/bkrd,bnkd->bkrn/dot_general | solution.py:26
  479.4 7.0 %reshape.65 = bf16[4096,4,128]{2,1,0:T(4,128)(2,1)} reshape(bf16[1,4096,512]{2,1,0:T(8,128)(2,1)} %get-tuple-element.23) | data formatting | bytes 8388608 | tf_op jit(solution)/shard_map/reshape.5
  486.3 54.0 %fusion.9 = f32[1,4,2048,128]{3,2,1,0:T(8,128)} fusion(bf16[4096,4,128]{2,1,0:T(4,128)(2,1)} %reshape.65, f32[4,2048,4096]{2,1,0:T(8,128)} %get-tuple-element.29, f32[4,2048]{1,0:T(4,128)S(1)} %broadcast_maximum_fusion, pred[2048,4096]{1,0:T(8,128)(4,1)} %iota_compare_fusion), kind=kOutput, calls=%fused_computation.11 | convolution fusion | flops 8757706752 | bytes 151027712 | tf_op jit(solution)/shard_map/cond/branch_1_fun/bkrn,bnkd->bkrd/dot_general | solution.py:35
  540.3 44.5 %fusion.2 = f32[4,2048]{1,0:T(4,128)} fusion(f32[4,2048,4096]{2,1,0:T(8,128)} %get-tuple-element.29, f32[4,2048]{1,0:T(4,128)S(1)} %broadcast_maximum_fusion, pred[2048,4096]{1,0:T(8,128)(4,1)} %iota_compare_fusion), kind=kLoop, calls=%fused_computation.4 | loop fusion | flops 167763968 | bytes 142671872 | tf_op jit(solution)/shard_map/cond/branch_1_fun/reduce_sum | solution.py:34
  584.9 2.9 divide_convert_fusion
  587.7 2.3 copy.16
  590.1 14.5 %convolution_convert_fusion = bf16[512,4096]{1,0:T(8,128)(2,1)} fusion(bf16[512,2048]{0,1:T(8,128)(2,1)} %bitcast.36, bf16[2048,4096]{1,0:T(8,128)(2,1)} %all-gather.20.cloned.1.call-done), kind=kOutput, calls=%fused_computation.22 | convolution fusion | flops 8592031744 | bytes 23068672 | tf_op jit(solution)/shard_map/dot_general | solution.py:101
  604.6 53.6 %reduce-scatter.2.cloned.1.call-done = bf16[512,2048]{1,0:T(8,128)(2,1)} async-done(((bf16[512,4096]{1,0:T(8,128)(2,1)}), bf16[512,2048]{1,0:T(8,128)(2,1)}) %reduce-scatter.2.cloned.1.call-update) | async-done | bytes 2097168 | tf_op jit(solution)/shard_map/reduce_scatter | solution.py:102
  (33 shorter events, 10.4 us)
Async XLA Ops:
  6.5 110.6 %copy-start.3 = (f32[4096]{0:T(1024)S(1)}, f32[4096]{0:T(1024)}, u32[]{:S(2)}) copy-start(f32[4096]{0:T(1024)} %param.9) | copy-start | bytes 49156
  6.5 61.8 %all-gather.8.cloned.1.call-start = ((), (), s32[]{:S(2)}) async-start(), calls=%async_computation.1 | async-start | bytes 6291456 | tf_op jit(solution)/shard_map/all_gather | solution.py:48
  7.3 109.9 %all-gather.12.cloned.1.call-start = ((), (), s32[]{:S(2)}) async-start(), calls=%async_computation.3 | async-start | bytes 4718592 | tf_op jit(solution)/shard_map/all_gather | solution.py:55
  8.0 156.7 %all-gather.16.cloned.1.call-start = ((), (), s32[]{:S(2)}) async-start(), calls=%async_computation.5 | async-start | bytes 4718592 | tf_op jit(solution)/shard_map/all_gather | solution.py:56
  8.7 307.2 %all-gather.10.cloned.1.call-start = ((), (), s32[]{:S(2)}) async-start(), calls=%async_computation.2 | async-start | bytes 18874368 | tf_op jit(solution)/shard_map/all_gather | solution.py:54
  9.3 353.5 %all-gather.14.cloned.1.call-start = ((), (), s32[]{:S(2)}) async-start(), calls=%async_computation.4 | async-start | bytes 4718592 | tf_op jit(solution)/shard_map/all_gather | solution.py:84
  123.0 14.1 %collective-permute-start = (bf16[1,512,512]{2,1,0:T(8,128)(2,1)S(1)}, bf16[1,512,512]{2,1,0:T(8,128)(2,1)S(1)}, u32[]{:S(2)}, u32[]{:S(2)}) collective-permute-start(bf16[1,512,512]{2,1,0:T(8,128)(2,1)S(1)} %fusion.20), channel_id=1, source_target_pairs={{0,16},{16,0},{1,17},{17,1},{2,18},{18,2},{3,19},{19,3},{4,20},{20... | collective-permute-start | bytes 1572872 | tf_op jit(solution)/shard_map/ppermute | solution.py:16
  137.1 0.8 copy-start.1
  138.0 272.2 %all-gather.18.cloned.1.call-start = ((), (), s32[]{:S(2)}) async-start(), calls=%async_computation.6 | async-start | bytes 4718592 | tf_op jit(solution)/shard_map/all_gather | solution.py:85
  170.5 14.1 %collective-permute-start.1 = (bf16[1,512,512]{2,1,0:T(8,128)(2,1)S(1)}, bf16[1,512,512]{2,1,0:T(8,128)(2,1)S(1)}, u32[]{:S(2)}, u32[]{:S(2)}) collective-permute-start(bf16[1,512,512]{2,1,0:T(8,128)(2,1)S(1)} %fusion.21), channel_id=1, source_target_pairs={{0,16},{16,0},{1,17},{17,1},{2,18},{18,2},{3,19},{19,3},{4,20},{20... | collective-permute-start | bytes 1572872 | tf_op jit(solution)/shard_map/ppermute | solution.py:16
  184.6 0.8 copy-start.2
  185.5 404.6 %all-gather.20.cloned.1.call-start = ((), (), s32[]{:S(2)}) async-start(), calls=%async_computation.7 | async-start | bytes 18874368 | tf_op jit(solution)/shard_map/all_gather | solution.py:57
  186.2 472.0 %reduce-scatter.2.cloned.1.call-start = ((), (), s32[]{:S(2)}) async-start(), calls=%async_computation.8 | async-start | bytes 6291456 | tf_op jit(solution)/shard_map/reduce_scatter | solution.py:102
  410.2 18.0 %copy-start = (bf16[1,4,4,512,128]{4,3,2,1,0:T(8,128)(2,1)S(1)}, bf16[1,4,4,512,128]{4,3,2,1,0:T(8,128)(2,1)}, u32[]{:S(2)}) copy-start(bf16[1,4,4,512,128]{4,3,2,1,0:T(8,128)(2,1)} %get-tuple-element.21) | copy-start | bytes 6291460 | tf_op jit(solution)/shard_map/cond
Sparse Core Ops, SparseCore 0:
  8.9 59.4 all-gather.7
  70.0 47.1 all-gather.11
  118.8 45.8 all-gather.15
  166.1 149.8 all-gather.9
  317.4 45.3 all-gather.13
  364.3 45.8 all-gather.17
  411.8 149.8 all-gather.19
  604.7 53.4 reduce-scatter.1
where the time goes:
time: 666 us; the launch traced here: 665 us
  waiting for transfers between devices  418 us (63%)
  matrix products  146 us (22%)
  other arithmetic  61.5 us (9%)
  local copies, waits for them, and re-layouts  23.1 us (3%)
  between operations  13.5 us (2%)
    all_gather x1, waiting for transfers between devices, body(): lax.all_gather(query_weight, 'seq', axis=0, tiled=True)  130 us
    all_gather x1, waiting for transfers between devices, body(): gathered = lax.all_gather(hidden, 'tensor', axis=3, tiled=True)  59 us
    dot_general x1, matrix products, online_update(): jnp.einsum('bkrn,bnkd->bkrd', expo.astype(jnp.bfloat16), value_heads, pre...  54 us
    reduce_scatter x1, waiting for transfers between devices, body(): lax.psum_scatter(partial_out.astype(jnp.bfloat16), 'tensor', scatter_dime...  53.6 us
    dot_general x1, matrix products, online_update(): jnp.einsum('bkrd,bnkd->bkrn', query_heads, key_heads, preferred_element_t...  51.1 us
    all_gather x1, waiting for transfers between devices, body(): lax.all_gather(partner_values, 'seq', axis=1, tiled=True)  47.4 us
    all_gather x1, waiting for transfers between devices, body(): lax.all_gather(key_weight, 'seq', axis=0, tiled=True)  45.7 us
    reduce_sum x1, other arithmetic, online_update(): totals = jnp.sum(expo, axis=-1)  44.5 us
  transfers between devices with their start and end apart: 10, of which 9 were waited for; matrix products, arithmetic and copies ran while one was open for 32% of the time, Pallas kernels for 0%

commit v1 on v0

--- a/solution.py
+++ b/solution.py
@@ -4,6 +4,27 @@
 from jax.sharding import PartitionSpec as P
 
 HEAD_DIM = 128
+
+
+def mix_row(base_x):
+    h_now = lax.axis_size("seq")
+    e_next, latest, current_block = (h_now, lax.axis_index("seq"), base_x.shape[0])
+    left_arr = jnp.zeros(
+        [at * e_next if dd == 0 else at for dd, at in enumerate(base_x.shape)], base_x.dtype
+    )
+    known = lax.dynamic_update_slice_in_dim(left_arr, base_x, latest * current_block, axis=0)
+    row_out = aux = base_x
+    for b in range(1, e_next // 2 + 1):
+        row_out = lax.ppermute(row_out, "seq", [(dd, (dd + 1) % e_next) for dd in range(e_next)])
+        known = lax.dynamic_update_slice_in_dim(
+            known, row_out, (latest - b) % e_next * current_block, axis=0
+        )
+        if 2 * b < e_next:
+            aux = lax.ppermute(aux, "seq", [(dd, (dd - 1) % e_next) for dd in range(e_next)])
+            known = lax.dynamic_update_slice_in_dim(
+                known, aux, (latest + b) % e_next * current_block, axis=0
+            )
+    return known
 
 
 def swapped(block, axis, stride):
@@ -51,7 +72,7 @@
     inverse_rms = lax.rsqrt(jnp.mean(flat_rows * flat_rows, axis=1, keepdims=True) + 1e-05)
     normed = (flat_rows * inverse_rms * norm_gain).astype(jnp.bfloat16)
     full_query, full_key, full_value, full_out = (
-        lax.all_gather(query_weight, "seq", axis=0, tiled=True),
+        mix_row(query_weight),
         lax.all_gather(key_weight, "seq", axis=0, tiled=True),
         lax.all_gather(value_projection_weight, "seq", axis=0, tiled=True),
         lax.all_gather(out_weight, "seq", axis=1, tiled=True),

time: 666 us -> 805 us (1.21)
  waiting for transfers between devices: 418 us -> 541 us
  local copies, waits for them, and re-layouts: 23.1 us -> 36.8 us
  starting transfers between devices: 3.53 us -> 13 us
    ppermute x0 -> x7, waiting for transfers between devices: none -> 299 us  [the longest x4 293 us: mix_row(): lax.ppermute(row_out, 'seq', [(dd, (dd + 1) % e_next) for dd in range(e_n...]
    all_gather x1 -> x0, waiting for transfers between devices: 130 us -> none  [body(): lax.all_gather(query_weight, 'seq', axis=0, tiled=True)]
    all_gather x1, waiting for transfers between devices: 47.4 us -> 0.01 us  [body(): lax.all_gather(partner_values, 'seq', axis=1, tiled=True)]
    reduce_scatter x1, waiting for transfers between devices: 53.6 us -> 82.3 us  [body(): lax.psum_scatter(partial_out.astype(jnp.bfloat16), 'tensor', scatter_dime...]
    all_gather x1, waiting for transfers between devices: 27.1 us -> 0.01 us  [body(): lax.all_gather(partner_keys, 'seq', axis=1, tiled=True)]
    ppermute x0 -> x7, starting transfers between devices: none -> 9.69 us  [the longest x3 9.62 us: mix_row(): lax.ppermute(aux, 'seq', [(dd, (dd - 1) % e_next) for dd in range(e_next)])]
    dynamic_update_slice x0 -> x8, local copies, waits for them, and re-layouts: none -> 8.7 us  [the longest x4 4.26 us: mix_row(): lax.dynamic_update_slice_in_dim(known, row_out, (latest - b) % e_next * c...]
  transfers between devices with their start and end apart: 10 -> 16, of which waited for: 9 -> 11; matrix products, arithmetic and copies ran while one was open for 32% -> 27% of each run, Pallas kernels for 0% -> 0%
where the time goes in v1:
time: 805 us
  waiting for transfers between devices  541 us (67%)
  matrix products  139 us (17%)
  other arithmetic  60.8 us (8%)
  local copies, waits for them, and re-layouts  36.8 us (5%)
  between operations  13.7 us (2%)
  starting transfers between devices  13 us (2%)
    ppermute x4, waiting for transfers between devices, mix_row(): lax.ppermute(row_out, 'seq', [(dd, (dd + 1) % e_next) for dd in range(e_n...  293 us
    reduce_scatter x1, waiting for transfers between devices, body(): lax.psum_scatter(partial_out.astype(jnp.bfloat16), 'tensor', scatter_dime...  82.3 us
    all_gather x1, waiting for transfers between devices, body(): gathered = lax.all_gather(hidden, 'tensor', axis=3, tiled=True)  59.6 us
    dot_general x1, matrix products, online_update(): jnp.einsum('bkrn,bnkd->bkrd', expo.astype(jnp.bfloat16), value_heads, pre...  53.4 us
    dot_general x1, matrix products, online_update(): jnp.einsum('bkrd,bnkd->bkrn', query_heads, key_heads, preferred_element_t...  49.4 us
    all_gather x1, waiting for transfers between devices, body(): lax.all_gather(key_weight, 'seq', axis=0, tiled=True)  45.7 us
    reduce_sum x1, other arithmetic, online_update(): totals = jnp.sum(expo, axis=-1)  44.6 us
    all_gather x1, waiting for transfers between devices, body(): lax.all_gather(value_projection_weight, 'seq', axis=0, tiled=True)  26.6 us
  transfers between devices with their start and end apart: 16, of which 11 were waited for; matrix products, arithmetic and copies ran while one was open for 27% of the time, Pallas kernels for 0%

profile of v1, /device:TPU:0, one launch (start us, length us, event | category | flops | bytes accessed | tf_op | source)
XLA Modules:
  0.0 804.9 jit_solution(3488407843064601428)
XLA Ops:
  8.8 59.6 %all-gather.7.cloned.1.call-done = bf16[1,1,512,4096]{3,2,1,0:T(8,128)(2,1)} async-done(((bf16[1,1,512,2048]{3,2,1,0:T(8,128)(2,1)}), bf16[1,1,512,4096]{3,2,1,0:T(8,128)(2,1)}) %all-gather.7.cloned.1.call-update) | async-done | bytes 4194320 | tf_op jit(solution)/shard_map/all_gather | solution.py:69
  71.5 45.7 %all-gather.9.cloned.1.call-done = bf16[4096,512]{1,0:T(8,128)(2,1)} async-done(((bf16[512,512]{1,0:T(8,128)(2,1)}), bf16[4096,512]{1,0:T(8,128)(2,1)}) %all-gather.9.cloned.1.call-update) | async-done | bytes 4194320 | tf_op jit(solution)/shard_map/all_gather | solution.py:76
  117.2 5.9 fusion.20
  124.6 12.6 %collective-permute-done.7 = bf16[1,512,512]{2,1,0:T(8,128)(2,1)S(1)} collective-permute-done((bf16[1,512,512]{2,1,0:T(8,128)(2,1)S(1)}, bf16[1,512,512]{2,1,0:T(8,128)(2,1)S(1)}, u32[]{:S(2)}, u32[]{:S(2)}) %collective-permute-start.7) | collective-permute-done | bytes 524320 | tf_op jit(solution)/shard_map/ppermute | solution.py:37
  138.1 26.6 %all-gather.13.cloned.1.call-done = bf16[4096,512]{1,0:T(8,128)(2,1)} async-done(((bf16[512,512]{1,0:T(8,128)(2,1)}), bf16[4096,512]{1,0:T(8,128)(2,1)}) %all-gather.13.cloned.1.call-update) | async-done | bytes 4194320 | tf_op jit(solution)/shard_map/all_gather | solution.py:77
  164.7 5.8 fusion.21
  172.1 12.6 %collective-permute-done.8 = bf16[1,512,512]{2,1,0:T(8,128)(2,1)S(1)} collective-permute-done((bf16[1,512,512]{2,1,0:T(8,128)(2,1)S(1)}, bf16[1,512,512]{2,1,0:T(8,128)(2,1)S(1)}, u32[]{:S(2)}, u32[]{:S(2)}) %collective-permute-start.8) | collective-permute-done | bytes 524320 | tf_op jit(solution)/shard_map/ppermute | solution.py:37
  186.2 3.5 collective-permute-start.1
  189.7 77.2 %collective-permute-done = bf16[512,2048]{1,0:T(8,128)(2,1)S(1)} collective-permute-done((bf16[512,2048]{1,0:T(8,128)(2,1)S(1)}, bf16[512,2048]{1,0:T(8,128)(2,1)S(1)}, u32[]{:S(2)}, u32[]{:S(2)}) %collective-permute-start) | collective-permute-done | bytes 2097184 | tf_op jit(solution)/shard_map/ppermute | solution.py:18
  270.5 69.5 %collective-permute-done.2 = bf16[512,2048]{1,0:T(8,128)(2,1)S(1)} collective-permute-done((bf16[512,2048]{1,0:T(8,128)(2,1)S(1)}, bf16[512,2048]{1,0:T(8,128)(2,1)S(1)}, u32[]{:S(2)}, u32[]{:S(2)}) %collective-permute-start.2) | collective-permute-done | bytes 2097184 | tf_op jit(solution)/shard_map/ppermute | solution.py:18
  340.0 6.8 collective-permute-done.3
  346.8 3.8 collective-permute-start.5
  350.6 82.7 %collective-permute-done.4 = bf16[512,2048]{1,0:T(8,128)(2,1)} collective-permute-done((bf16[512,2048]{1,0:T(8,128)(2,1)S(1)}, bf16[512,2048]{1,0:T(8,128)(2,1)}, u32[]{:S(2)}, u32[]{:S(2)}) %collective-permute-start.4) | collective-permute-done | bytes 2097184 | tf_op jit(solution)/shard_map/ppermute | solution.py:18
  443.9 63.2 %collective-permute-done.6 = bf16[512,2048]{1,0:T(8,128)(2,1)} collective-permute-done((bf16[512,2048]{1,0:T(8,128)(2,1)}, bf16[512,2048]{1,0:T(8,128)(2,1)}, u32[]{:S(2)}, u32[]{:S(2)}) %collective-permute-start.6) | collective-permute-done | bytes 2097184 | tf_op jit(solution)/shard_map/ppermute | solution.py:18
  509.0 10.2 %convolution_convert_fusion.1 = bf16[512,2048]{1,0:T(8,128)(2,1)} fusion(bf16[4096,2048]{1,0:T(8,128)(2,1)S(1)} %constant_dynamic-update-slice_fusion, bf16[1,1,512,4096]{3,2,1,0:T(8,128)(2,1)S(1)} %copy-done, f32[4096]{0:T(1024)S(1)} %copy-done.11, f32[512]{0:T(512)S(1)} %add_rsqrt_fusion), kind=kOutput, calls=%fused_computation.24 | convolution fusion | flops 8599371776 | bytes 23087104 | tf_op jit(solution)/shard_map/dot_general | solution.py:80
  524.5 171.5 %conditional.1 = (f32[1,4,2048]{2,1,0:T(4,128)}, f32[1,4,2048,128]{3,2,1,0:T(8,128)}) conditional(s32[]{:T(128)} %convert_element_type.33, () %tuple.13, (s32[]{:T(128)}, s32[4,512]{1,0:T(4,128)S(1)}, bf16[1,4,4,512,128]{4,3,2,1,0:T(8,128)(2,1)}, bf16[1,4096,512]{2,1,0:T(8,128)(2,1)}, bf16[1,4096,512]{2,1,0:T(8,128)(2,1)}) %tuple.32), branch_computations={%region_1.2_spmd, %region_2.5_spmd} | conditional | flops 17624459264 | bytes 476291136 | solution.py:115
  524.5 10.2 %iota_compare_fusion = pred[2048,4096]{1,0:T(8,128)(4,1)} fusion(s32[2048]{0:T(1024)S(1)} %bitcast.37), kind=kLoop, calls=%fused_computation.7 | loop fusion | flops 8388608 | bytes 8396800 | tf_op jit(solution)/shard_map/cond/branch_1_fun/le | solution.py:51
  534.7 6.9 reshape.64
  541.6 49.4 %fusion = (f32[4,2048]{1,0:T(4,128)S(1)}, f32[4,2048,4096]{2,1,0:T(8,128)}) fusion(pred[2048,4096]{1,0:T(8,128)(4,1)} %iota_compare_fusion, bf16[4,2048,128]{2,1,0:T(8,128)(2,1)S(1)} %bitcast.35, bf16[4096,4,128]{2,1,0:T(4,128)(2,1)} %reshape.64), kind=kOutput, calls=%fused_computation.2 | convolution fusion | flops 8690589696 | bytes 148930560 | tf_op jit(solution)/shard_map/cond/branch_1_fun/bkrd,bnkd->bkrn/dot_general | solution.py:47
  591.1 6.9 reshape.65
  598.0 53.4 %fusion.9 = f32[1,4,2048,128]{3,2,1,0:T(8,128)} fusion(bf16[4096,4,128]{2,1,0:T(4,128)(2,1)} %reshape.65, f32[4,2048,4096]{2,1,0:T(8,128)} %get-tuple-element.29, f32[4,2048]{1,0:T(4,128)S(1)} %broadcast_maximum_fusion, pred[2048,4096]{1,0:T(8,128)(4,1)} %iota_compare_fusion), kind=kOutput, calls=%fused_computation.11 | convolution fusion | flops 8757706752 | bytes 151027712 | tf_op jit(solution)/shard_map/cond/branch_1_fun/bkrn,bnkd->bkrd/dot_general | solution.py:56
  651.4 44.6 %fusion.2 = f32[4,2048]{1,0:T(4,128)} fusion(f32[4,2048,4096]{2,1,0:T(8,128)} %get-tuple-element.29, f32[4,2048]{1,0:T(4,128)S(1)} %broadcast_maximum_fusion, pred[2048,4096]{1,0:T(8,128)(4,1)} %iota_compare_fusion), kind=kLoop, calls=%fused_computation.4 | loop fusion | flops 167763968 | bytes 142671872 | tf_op jit(solution)/shard_map/cond/branch_1_fun/reduce_sum | solution.py:55
  701.2 14.5 %convolution_convert_fusion = bf16[512,4096]{1,0:T(8,128)(2,1)} fusion(bf16[512,2048]{0,1:T(8,128)(2,1)} %bitcast.36, bf16[2048,4096]{1,0:T(8,128)(2,1)} %all-gather.17.cloned.1.call-done), kind=kOutput, calls=%fused_computation.22 | convolution fusion | flops 8592031744 | bytes 23068672 | tf_op jit(solution)/shard_map/dot_general | solution.py:122
  715.8 82.3 %reduce-scatter.2.cloned.1.call-done = bf16[512,2048]{1,0:T(8,128)(2,1)} async-done(((bf16[512,4096]{1,0:T(8,128)(2,1)}), bf16[512,2048]{1,0:T(8,128)(2,1)}) %reduce-scatter.2.cloned.1.call-update) | async-done | bytes 2097168 | tf_op jit(solution)/shard_map/reduce_scatter | solution.py:123
  (69 shorter events, 37.3 us)
Async XLA Ops:
  6.5 61.8 %all-gather.7.cloned.1.call-start = ((), (), s32[]{:S(2)}) async-start(), calls=%async_computation.1 | async-start | bytes 6291456 | tf_op jit(solution)/shard_map/all_gather | solution.py:69
  7.3 109.9 %all-gather.9.cloned.1.call-start = ((), (), s32[]{:S(2)}) async-start(), calls=%async_computation.2 | async-start | bytes 4718592 | tf_op jit(solution)/shard_map/all_gather | solution.py:76
  8.0 156.7 %all-gather.13.cloned.1.call-start = ((), (), s32[]{:S(2)}) async-start(), calls=%async_computation.4 | async-start | bytes 4718592 | tf_op jit(solution)/shard_map/all_gather | solution.py:77
  8.7 515.7 %all-gather.11.cloned.1.call-start = ((), (), s32[]{:S(2)}) async-start(), calls=%async_computation.3 | async-start | bytes 4718592 | tf_op jit(solution)/shard_map/all_gather | solution.py:105
  71.5 93.2 %copy-start.11 = (f32[4096]{0:T(1024)S(1)}, f32[4096]{0:T(1024)}, u32[]{:S(2)}) copy-start(f32[4096]{0:T(1024)} %param.9) | copy-start | bytes 49156
  123.0 14.1 %collective-permute-start.7 = (bf16[1,512,512]{2,1,0:T(8,128)(2,1)S(1)}, bf16[1,512,512]{2,1,0:T(8,128)(2,1)S(1)}, u32[]{:S(2)}, u32[]{:S(2)}) collective-permute-start(bf16[1,512,512]{2,1,0:T(8,128)(2,1)S(1)} %fusion.20), channel_id=1, source_target_pairs={{0,16},{16,0},{1,17},{17,1},{2,18},{18,2},{3,19},{19,3},{4,20},{20... | collective-permute-start | bytes 1572872 | tf_op jit(solution)/shard_map/ppermute | solution.py:37
  138.0 48.1 %copy-start.1 = (bf16[512,2048]{1,0:T(8,128)(2,1)S(1)}, bf16[512,2048]{1,0:T(8,128)(2,1)}, u32[]{:S(2)}) copy-start(bf16[512,2048]{1,0:T(8,128)(2,1)} %param.10) | copy-start | bytes 6291460
  138.0 386.4 %all-gather.15.cloned.1.call-start = ((), (), s32[]{:S(2)}) async-start(), calls=%async_computation.5 | async-start | bytes 4718592 | tf_op jit(solution)/shard_map/all_gather | solution.py:106
  170.5 14.1 %collective-permute-start.8 = (bf16[1,512,512]{2,1,0:T(8,128)(2,1)S(1)}, bf16[1,512,512]{2,1,0:T(8,128)(2,1)S(1)}, u32[]{:S(2)}, u32[]{:S(2)}) collective-permute-start(bf16[1,512,512]{2,1,0:T(8,128)(2,1)S(1)} %fusion.21), channel_id=1, source_target_pairs={{0,16},{16,0},{1,17},{17,1},{2,18},{18,2},{3,19},{19,3},{4,20},{20... | collective-permute-start | bytes 1572872 | tf_op jit(solution)/shard_map/ppermute | solution.py:37
  185.5 515.8 %all-gather.17.cloned.1.call-start = ((), (), s32[]{:S(2)}) async-start(), calls=%async_computation.6 | async-start | bytes 18874368 | tf_op jit(solution)/shard_map/all_gather | solution.py:78
  186.1 612.0 %reduce-scatter.2.cloned.1.call-start = ((), (), s32[]{:S(2)}) async-start(), calls=%async_computation.7 | async-start | bytes 6291456 | tf_op jit(solution)/shard_map/reduce_scatter | solution.py:123
  186.1 80.7 %collective-permute-start = (bf16[512,2048]{1,0:T(8,128)(2,1)S(1)}, bf16[512,2048]{1,0:T(8,128)(2,1)S(1)}, u32[]{:S(2)}, u32[]{:S(2)}) collective-permute-start(bf16[512,2048]{1,0:T(8,128)(2,1)S(1)} %copy-done.1), channel_id=1, source_target_pairs={{0,2},{2,4},{4,6},{6,8},{8,10},{10,12},{12,14},{14,0},{1,3},{3,5},... | collective-permute-start | bytes 6291464 | tf_op jit(solution)/shard_map/ppermute | solution.py:18
  186.2 80.7 %collective-permute-start.1 = (bf16[512,2048]{1,0:T(8,128)(2,1)S(1)}, bf16[512,2048]{1,0:T(8,128)(2,1)S(1)}, u32[]{:S(2)}, u32[]{:S(2)}) collective-permute-start(bf16[512,2048]{1,0:T(8,128)(2,1)S(1)} %copy-done.1), channel_id=1, source_target_pairs={{0,14},{2,0},{4,2},{6,4},{8,6},{10,8},{12,10},{14,12},{1,15},{3,1}... | collective-permute-start | bytes 6291464 | tf_op jit(solution)/shard_map/ppermute | solution.py:23
  266.9 73.1 %collective-permute-start.2 = (bf16[512,2048]{1,0:T(8,128)(2,1)S(1)}, bf16[512,2048]{1,0:T(8,128)(2,1)S(1)}, u32[]{:S(2)}, u32[]{:S(2)}) collective-permute-start(bf16[512,2048]{1,0:T(8,128)(2,1)S(1)} %collective-permute-done), channel_id=1, source_target_pairs={{0,2},{2,4},{4,6},{6,8},{8,10},{10,12},{12,14},{14,0},{1,3},{3,5},... | collective-permute-start | bytes 6291464 | tf_op jit(solution)/shard_map/ppermute | solution.py:18
  268.2 71.8 %copy-start.4 = (bf16[512,2048]{1,0:T(8,128)(2,1)}, bf16[512,2048]{1,0:T(8,128)(2,1)S(1)}, u32[]{:S(2)}) copy-start(bf16[512,2048]{1,0:T(8,128)(2,1)S(1)} %collective-permute-done.1) | copy-start | bytes 6291460
  268.2 78.6 %collective-permute-start.3 = (bf16[512,2048]{1,0:T(8,128)(2,1)S(1)}, bf16[512,2048]{1,0:T(8,128)(2,1)}, u32[]{:S(2)}, u32[]{:S(2)}) collective-permute-start(bf16[512,2048]{1,0:T(8,128)(2,1)S(1)} %collective-permute-done.1), channel_id=1, source_target_pairs={{0,14},{2,0},{4,2},{6,4},{8,6},{10,8},{12,10},{14,12},{1,15},{3,1}... | collective-permute-start | bytes 6291464 | tf_op jit(solution)/shard_map/ppermute | solution.py:23
  340.0 6.8 copy-start.6
  340.0 93.3 %collective-permute-start.4 = (bf16[512,2048]{1,0:T(8,128)(2,1)S(1)}, bf16[512,2048]{1,0:T(8,128)(2,1)}, u32[]{:S(2)}, u32[]{:S(2)}) collective-permute-start(bf16[512,2048]{1,0:T(8,128)(2,1)S(1)} %collective-permute-done.2), channel_id=1, source_target_pairs={{0,2},{2,4},{4,6},{6,8},{8,10},{10,12},{12,14},{14,0},{1,3},{3,5},... | collective-permute-start | bytes 6291464 | tf_op jit(solution)/shard_map/ppermute | solution.py:18
  346.8 95.2 %collective-permute-start.5 = (bf16[512,2048]{1,0:T(8,128)(2,1)}, bf16[512,2048]{1,0:T(8,128)(2,1)}, u32[]{:S(2)}, u32[]{:S(2)}) collective-permute-start(bf16[512,2048]{1,0:T(8,128)(2,1)} %collective-permute-done.3), channel_id=1, source_target_pairs={{0,14},{2,0},{4,2},{6,4},{8,6},{10,8},{12,10},{14,12},{1,15},{3,1}... | collective-permute-start | bytes 6291464 | tf_op jit(solution)/shard_map/ppermute | solution.py:23
  433.3 73.8 %collective-permute-start.6 = (bf16[512,2048]{1,0:T(8,128)(2,1)}, bf16[512,2048]{1,0:T(8,128)(2,1)}, u32[]{:S(2)}, u32[]{:S(2)}) collective-permute-start(bf16[512,2048]{1,0:T(8,128)(2,1)} %collective-permute-done.4), channel_id=1, source_target_pairs={{0,2},{2,4},{4,6},{6,8},{8,10},{10,12},{12,14},{14,0},{1,3},{3,5},... | collective-permute-start | bytes 6291464 | tf_op jit(solution)/shard_map/ppermute | solution.py:18
  433.3 2.4 copy-start.3
  435.4 2.4 copy-start.7
  438.1 70.9 %copy-start = (bf16[1,1,512,4096]{3,2,1,0:T(8,128)(2,1)S(1)}, bf16[1,1,512,4096]{3,2,1,0:T(8,128)(2,1)}, u32[]{:S(2)}) copy-start(bf16[1,1,512,4096]{3,2,1,0:T(8,128)(2,1)} %all-gather.7.cloned.1.call-done) | copy-start | bytes 12582916
  524.5 17.1 %copy-start.8 = (bf16[1,4,4,512,128]{4,3,2,1,0:T(8,128)(2,1)S(1)}, bf16[1,4,4,512,128]{4,3,2,1,0:T(8,128)(2,1)}, u32[]{:S(2)}) copy-start(bf16[1,4,4,512,128]{4,3,2,1,0:T(8,128)(2,1)} %get-tuple-element.21) | copy-start | bytes 6291460 | tf_op jit(solution)/shard_map/cond
  (4 other events, 4.6 us)
Sparse Core Ops, SparseCore 0:
  8.9 59.4 all-gather.6
  70.0 47.1 all-gather.8
  118.8 45.8 all-gather.12
  166.1 60.0 all-gather.10
  227.6 77.5 all-gather.14
  306.6 231.2 all-gather.16
  715.9 82.0 reduce-scatter.1
